TPU v7x, 32 devices: a whole 2x2x4 slice. The times are simulated.
32 devices in a mesh: grp: 4 (over z), dir: 8 (over y, x, core).
Axes of the slice: x: 2, y: 2, z: 4, core: 2. Of those that a mesh axis runs over, the one named last changes fastest.
Arguments:
- incident: float32 [4, 256, 256, 128], P(None, ('grp', 'dir')), may hold values from -6 to 6
- currents_past: bfloat16 [2, 256, 256, 128], P(None, ('grp', 'dir')), may hold values from -6 to 6
- spectra_past: bfloat16 [2, 32, 1152, 128], P(None, ('grp', 'dir')), may hold values from -9 to 9
- self_inverse: bfloat16 [256, 256, 256], P(('grp', 'dir')), may hold values from -0.25 to 0.25
- near_blocks: bfloat16 [256, 6, 2, 256, 256], P(('grp', 'dir')), may hold values from -0.078125 to 0.078125
- neighbours: int32 [256, 6], P(('grp', 'dir')), may hold values from 0 to 255, as said below
- near_mask: int32 [256, 6], P(('grp', 'dir')), may hold values 0 or 1
- ray_out: bfloat16 [256, 1152], replicated, may hold values from -0.375 to 0.375
- ray_in: bfloat16 [1152, 256], replicated, may hold values from -0.1875 to 0.1875
- child_shift: float32 [8, 1152], replicated, may hold values from -1 to 1
- far_sources: int32 [32, 16], replicated, may hold values from 0 to 31
- far_delays: int32 [32, 16], replicated, may hold values from 1 to 2
- translation: float32 [32, 16, 1152], P(None, None, ('grp', 'dir')), may hold values from -0.75 to 0.75
Outputs:
- currents: bfloat16 [4, 256, 256, 128], P(None, ('grp', 'dir'))
Inputs may be any that keep to these rules, and one draw needn't show every extreme that they name: `neighbours`: the entry of group g names a group held by the same device as g, by the device just before it or by the one just after it, devices counted in the order grp then dir, each holding 8 consecutive groups.
All inputs are finite; a program needn't handle non-finite values. No bound on the sum of `near_mask` on one device may be relied on, other than what follows from the above.
Results may differ from a plain program's by a relative error of at most 0.0095.
Values may be sent and summed in bfloat16 or wider, within the bound.
A program may use at most 128 MiB of HBM per device.

v0:
```python
import functools

import jax
import jax.numpy as jnp
from jax import lax
from jax.experimental import pallas as pl
from jax.experimental.pallas import tpu as pltpu
from jax.sharding import PartitionSpec as P

MESH = pl.DeviceIdType.MESH
TILE = 16
MIB = 1 << 20
AXES = ("grp", "dir")


def dot(a, b):
    return jnp.dot(a, b, preferred_element_type=jnp.float32)


def march(
    sizes,
    table,
    incident,
    currents_past,
    spectra_past,
    self_inverse,
    near_blocks,
    ray_out_t,
    ray_in_t,
    shift_rows,
    shift_columns,
    slots,
    factors,
    out,
    *scratch,
):
    steps, lags, devices, per_row, groups, near_slots, kept = sizes
    scratch = list(scratch)
    times = lags + steps - 1
    curs = [scratch.pop(0) for _ in range(times)]
    bands = [scratch.pop(0) for _ in range(times)]
    leaving = [scratch.pop(0) for _ in range(steps - 1)]
    turned = [scratch.pop(0) for _ in range(steps)]
    arrived = [scratch.pop(0) for _ in range(steps)]
    (last, inc, inverse, blocks, project, test, acc, part, weights) = scratch[:9]
    (load_sem, own_sem, cur_send, cur_recv, band_send, band_recv, inc_send, inc_recv, out_sem) = scratch[9:]
    padded = bands[0].shape[1]
    depth = padded // TILE
    parents = devices
    wide = parents * TILE
    chunk = 8
    me = lax.axis_index("grp") * per_row + lax.axis_index("dir")

    def place(device):
        return (device // per_row, device % per_row)

    loads = [
        pltpu.make_async_copy(near_blocks, blocks, load_sem.at[0]),
        pltpu.make_async_copy(incident, inc, load_sem.at[1]),
        pltpu.make_async_copy(self_inverse, inverse, load_sem.at[2]),
    ]
    for lag in range(lags):
        slot = lags - 1 - lag
        loads.append(
            pltpu.make_async_copy(
                currents_past.at[lag], curs[slot].at[pl.ds(groups, groups)], load_sem.at[3 + lag]
            )
        )
        loads.append(
            pltpu.make_async_copy(spectra_past.at[lag, me], bands[slot].at[me], own_sem.at[lag])
        )
    for load in loads[1:] + loads[:1]:
        load.start()

    barrier = pltpu.get_barrier_semaphore()

    def greet(offset, carry):
        device = lax.rem(me + offset, devices)
        pl.semaphore_signal(barrier, inc=1, device_id=place(device), device_id_type=MESH)
        return carry

    lax.fori_loop(1, devices, greet, 0)
    pl.semaphore_wait(barrier, devices - 1)

    def neighbour_copies(source, slot):
        def copy(side):
            device = me + (1 if side == 0 else -1)
            return pltpu.make_async_remote_copy(
                src_ref=source,
                dst_ref=curs[slot].at[pl.ds(0 if side == 0 else 2 * groups, groups)],
                send_sem=cur_send.at[slot, side],
                recv_sem=cur_recv.at[slot, side],
                device_id=place(device),
                device_id_type=MESH,
            )

        return copy

    def start_neighbours(source, slot):
        copy = neighbour_copies(source, slot)

        @pl.when(me < devices - 1)
        def _():
            copy(0).start()

        @pl.when(me > 0)
        def _():
            copy(1).start()

    def wait_neighbours(slot):
        own = curs[slot].at[pl.ds(groups, groups)]
        copy = neighbour_copies(own, slot)

        @pl.when(me > 0)
        def _():
            copy(0).wait_recv()

        @pl.when(me < devices - 1)
        def _():
            copy(1).wait_recv()

    def finish_neighbours(slot):
        own = curs[slot].at[pl.ds(groups, groups)]
        copy = neighbour_copies(own, slot)

        @pl.when(me < devices - 1)
        def _():
            copy(0).wait_send()

        @pl.when(me > 0)
        def _():
            copy(1).wait_send()

    def post(source, target, send, recv, device):
        pltpu.make_async_remote_copy(
            src_ref=source,
            dst_ref=target.at[me],
            send_sem=send,
            recv_sem=recv,
            device_id=place(device),
            device_id_type=MESH,
        ).start()

    def drain(buffer, sem):
        most = buffer.at[pl.ds(0, devices - 1)]
        pltpu.make_async_copy(most, most, sem).wait()

    for lag in reversed(range(lags)):
        slot = lags - 1 - lag

        def first(offset, carry, lag=lag, slot=slot):
            device = lax.rem(me + offset, devices)
            post(
                spectra_past.at[lag, device],
                bands[slot],
                band_send.at[slot],
                band_recv.at[slot],
                device,
            )
            return carry

        lax.fori_loop(1, devices, first, 0)
    for lag in reversed(range(lags)):
        start_neighbours(currents_past.at[lag], lags - 1 - lag)

    for cur in curs:
        cur[3 * groups] = jnp.zeros(cur.shape[1:], cur.dtype)

    def build(o):
        lane = lax.broadcasted_iota(jnp.int32, (slots.shape[1], lags * wide), 1)
        chosen = (lane // TILE == slots[o]).astype(jnp.float32).astype(jnp.bfloat16)
        full = dot(factors[o], chosen)
        row = lax.broadcasted_iota(jnp.int32, full.shape, 0) % TILE
        column = lax.broadcasted_iota(jnp.int32, full.shape, 1) % TILE
        return jnp.where(row == column, full, 0.0).astype(jnp.bfloat16)

    if kept:

        def build_one(o, carry):
            full = build(o)
            for tile in range(depth):
                for lag in range(lags):
                    weights[tile, lag, pl.ds(pl.multiple_of(o * TILE, TILE), TILE), :] = full[
                        tile * TILE : (tile + 1) * TILE, lag * wide : (lag + 1) * wide
                    ]
            return carry

        lax.fori_loop(0, parents, build_one, 0)

    children = shift_rows.shape[0]
    unknowns = ray_out_t.shape[1]

    def build_ray(band, carry):
        rows = pl.ds(pl.multiple_of(band * padded, TILE), padded)
        value = ray_out_t[rows, :].astype(jnp.float32)
        shifts = shift_columns[rows, :]
        for child in range(children):
            project[rows, child * unknowns : (child + 1) * unknowns] = (
                value * shifts[:, child : child + 1]
            ).astype(jnp.bfloat16)
        return carry

    lax.fori_loop(0, devices, build_ray, 0)

    def build_test(piece, carry):
        rows = pl.ds(pl.multiple_of(piece * 32, 32), 32)
        value = ray_in_t[rows, :].astype(jnp.float32)
        for child in range(children):
            test[child, rows, :] = (value * shift_rows[child : child + 1, :]).astype(jnp.bfloat16)
        return carry

    lax.fori_loop(0, unknowns // 32, build_test, 0)

    def near_part(slot, lag, step, opening):
        def one(g, carry):
            total = inc[step, g] if opening else acc[g]
            for n in range(near_slots):
                total = total - dot(blocks[g, n, lag], curs[slot][table[g, n]])
            acc[g] = total
            return carry

        lax.fori_loop(0, groups, one, 0)

    def band_rows(slot, tile):
        return bands[slot][:, tile * TILE : (tile + 1) * TILE, :].reshape(wide, bands[slot].shape[2])

    def translate(step, slots_used, lag, final):
        source = [band_rows(slots_used[lag], tile) for tile in range(depth)]

        def one(piece, carry):
            turn = lax.rem(me // chunk + piece, parents // chunk)
            first_o = turn * chunk
            rows = pl.ds(pl.multiple_of(first_o * TILE, TILE), chunk * TILE)
            if not kept:
                built = [build(first_o + o) for o in range(chunk)]
            for tile in range(depth):
                if kept:
                    weight = weights[tile, lag, rows, :]
                else:
                    weight = jnp.concatenate(
                        [
                            b[tile * TILE : (tile + 1) * TILE, lag * wide : (lag + 1) * wide]
                            for b in built
                        ],
                        axis=0,
                    )
                got = dot(weight, source[tile])
                if not final:
                    part[tile, rows, :] = got
                else:
                    got = (got + part[tile, rows, :]).astype(jnp.bfloat16)
                    turned[step][pl.ds(first_o, chunk), tile * TILE : (tile + 1) * TILE, :] = (
                        got.reshape(chunk, TILE, got.shape[1])
                    )
            if final:
                send_chunk(turned[step], arrived[step], inc_send.at[step], inc_recv.at[step], first_o)
            return carry

        lax.fori_loop(0, parents // chunk, one, 0)

    def send_chunk(source, target, send, recv, begin):
        def one(offset, carry):
            device = begin + lax.rem(me + offset, chunk)

            @pl.when(device != me)
            def _():
                post(source.at[device], target, send, recv, device)

            @pl.when(device == me)
            def _():
                target[me] = source[me]

            return carry

        lax.fori_loop(0, chunk, one, 0)

    def outgoing(step, slot):
        stacked = curs[slot][pl.ds(groups, groups)].reshape(children * unknowns, -1)

        def one(piece, carry):
            turn = lax.rem(me // chunk + piece, devices // chunk)
            begin = turn * chunk
            rows = pl.ds(pl.multiple_of(begin * padded, TILE), chunk * padded)
            got = dot(project[rows, :], stacked).astype(jnp.bfloat16)
            leaving[step][pl.ds(begin, chunk)] = got.reshape(chunk, padded, got.shape[1])
            send_chunk(leaving[step], bands[slot], band_send.at[slot], band_recv.at[slot], begin)
            return carry

        lax.fori_loop(0, devices // chunk, one, 0)

    for load in loads:
        load.wait()
    results = []
    for step in range(steps):
        newest = lags + step - 1
        oldest = newest - 1
        if step == 0:
            drain(bands[oldest], band_recv.at[oldest])
            wait_neighbours(oldest)
        near_part(oldest, 1, step, True)
        translate(step, [newest, oldest], 1, False)
        drain(bands[newest], band_recv.at[newest])
        translate(step, [newest, oldest], 0, True)
        wait_neighbours(newest)
        near_part(newest, 0, step, False)
        drain(arrived[step], inc_recv.at[step])
        slot = lags + step
        target, base = (curs[slot], groups) if step + 1 < steps else (last, 0)
        received = arrived[step][...].reshape(devices * padded, -1)

        def solve(g, carry, target=target, base=base, received=received):
            drive = (acc[g] - dot(test[g], received)).astype(jnp.bfloat16)
            target[base + g] = dot(inverse[g], drive).astype(jnp.bfloat16)
            return carry

        lax.fori_loop(0, groups, solve, 0)
        own = target.at[pl.ds(base, groups)]
        results.append(pltpu.make_async_copy(own, out.at[step], out_sem.at[step]))
        if step + 1 < steps:
            start_neighbours(own, slot)
            outgoing(step, slot)
        results[-1].start()
    for slot in range(times):
        drain(bands[slot], band_send.at[slot])
        finish_neighbours(slot)
        if slot == times - 1:
            pass
    for step in range(steps):
        drain(arrived[step], inc_send.at[step])
        results[step].wait()


def on_device(
    devices,
    per_row,
    incident,
    currents_past,
    spectra_past,
    self_inverse,
    near_blocks,
    neighbours,
    near_mask,
    ray_out,
    ray_in,
    child_shift,
    far_sources,
    far_delays,
    translation,
):
    steps, groups, unknowns, columns = incident.shape
    lags = currents_past.shape[0]
    near_slots = neighbours.shape[1]
    children, rays = child_shift.shape
    parents = far_sources.shape[0]
    band = rays // devices
    padded = -(-band // TILE) * TILE
    depth = padded // TILE
    wide = parents * TILE
    bf16 = jnp.bfloat16
    first_group = (lax.axis_index(AXES) - 1) * groups
    table = jnp.where(near_mask > 0, neighbours - first_group, 3 * groups)
    spread = ((0, 0), (0, padded - band), (0, 0))

    def by_band(rows):
        width = rows.shape[1]
        return jnp.pad(rows.reshape(devices, band, width), spread).reshape(devices * padded, width)

    ray_out_t = by_band(ray_out.T)
    ray_in_t = by_band(ray_in).T
    shift_columns = by_band(child_shift.T)
    shift_rows = shift_columns.T
    past = jnp.pad(
        spectra_past.reshape(lags, devices, band, columns),
        ((0, 0), (0, 0), (0, padded - band), (0, 0)),
    )
    slots = ((far_delays - 1) * parents + far_sources)[:, :, None]
    factors = jnp.pad(jnp.swapaxes(translation, 1, 2), spread).astype(bf16)
    kept = depth * lags * wide * wide * 2 <= 12 * MIB
    times = lags + steps - 1
    slabs = pltpu.VMEM((devices, padded, columns), bf16)
    scratch = (
        [pltpu.VMEM((3 * groups + 1, unknowns, columns), bf16)] * times
        + [slabs] * times
        + [slabs] * (steps - 1)
        + [slabs] * steps
        + [slabs] * steps
        + [
            pltpu.VMEM((groups, unknowns, columns), bf16),
            pltpu.VMEM(incident.shape, jnp.float32),
            pltpu.VMEM(self_inverse.shape, bf16),
            pltpu.VMEM(near_blocks.shape, bf16),
            pltpu.VMEM((devices * padded, children * unknowns), bf16),
            pltpu.VMEM((children, unknowns, devices * padded), bf16),
            pltpu.VMEM((groups, unknowns, columns), jnp.float32),
            pltpu.VMEM((depth, wide, columns), jnp.float32),
            pltpu.VMEM((depth, lags, wide, wide) if kept else (1, 1, TILE, 128), bf16),
            pltpu.SemaphoreType.DMA((3 + lags,)),
            pltpu.SemaphoreType.DMA((lags,)),
            pltpu.SemaphoreType.DMA((times, 2)),
            pltpu.SemaphoreType.DMA((times, 2)),
            pltpu.SemaphoreType.DMA((times,)),
            pltpu.SemaphoreType.DMA((times,)),
            pltpu.SemaphoreType.DMA((steps,)),
            pltpu.SemaphoreType.DMA((steps,)),
            pltpu.SemaphoreType.DMA((steps,)),
        ]
    )
    sizes = (steps, lags, devices, per_row, groups, near_slots, kept)
    far = pl.BlockSpec(memory_space=pl.ANY)
    near = pl.BlockSpec(memory_space=pltpu.VMEM)
    return pl.pallas_call(
        functools.partial(march, sizes),
        out_shape=jax.ShapeDtypeStruct(incident.shape, bf16),
        in_specs=[pl.BlockSpec(memory_space=pltpu.SMEM)] + [far] * 5 + [near] * 6,
        out_specs=far,
        scratch_shapes=scratch,
        compiler_params=pltpu.CompilerParams(
            collective_id=0, has_side_effects=True, vmem_limit_bytes=63 * MIB
        ),
    )(
        table,
        incident,
        currents_past,
        past,
        self_inverse,
        near_blocks,
        ray_out_t,
        ray_in_t,
        shift_rows,
        shift_columns,
        slots,
        factors,
    )


def solution(mesh):
    in_specs = (
        P(None, AXES, None, None),
        P(None, AXES, None, None),
        P(None, AXES, None, None),
        P(AXES, None, None),
        P(AXES, None, None, None, None),
        P(AXES, None),
        P(AXES, None),
        P(),
        P(),
        P(),
        P(),
        P(),
        P(None, None, AXES),
    )
    per_row = mesh.shape["dir"]
    devices = mesh.shape["grp"] * per_row
    return jax.shard_map(
        functools.partial(on_device, devices, per_row),
        mesh=mesh,
        in_specs=in_specs,
        out_specs=P(None, AXES, None, None),
        check_vma=False,
    )
```

profile of v0, /device:TPU:16, one launch (start us, length us, event | category | flops | bytes accessed | tf_op | source)
XLA Modules:
  0.0 170.2 jit_solution(17405360082283818653)
XLA Ops:
  0.0 1.4 subtract_select_fusion.table
  1.4 0.7 add_bitcast_fusion
  2.1 0.9 reshape.26
  3.0 1.0 convert.5
  4.0 0.0 copy-start.2
  4.0 0.3 copy.34
  4.3 0.8 pad.24.factors
  5.1 0.9 copy.36.slots
  6.0 0.3 copy.33
  6.3 0.1 pad.23
  6.4 0.0 copy-start.3
  6.4 0.9 copy.35.shift_rows
  7.3 0.0 copy-done.1
  7.3 4.9 %copy.29 = bf16[2,1,1152,128]{3,0,2,1:T(2,128)(2,1)S(1)} copy(bf16[2,1,1152,128]{3,2,1,0:T(8,128)(2,1)S(1)} %copy-done.1) | data formatting | bytes 1179648 | tf_op args[2]
  12.2 0.1 copy.30
  12.3 1.0 pad.20.spectra_past
  13.2 0.2 copy.31
  13.5 0.1 reshape.22
  13.6 1.0 pad.21
  14.5 0.1 reshape.24
  14.7 0.1 pad.22
  14.7 1.2 copy.32
  15.9 151.1 %shard_map.127 = bf16[4,8,256,128]{3,2,1,0:T(8,128)(2,1)} custom-call(s32[8,6]{1,0:T(8,128)} %subtract_select_fusion.table, f32[4,8,256,128]{3,2,1,0:T(8,128)} %incident.1, bf16[2,8,256,128]{3,2,1,0:T(8,128)(2,1)} %currents_past.1, bf16[2,32,48,128]{3,2,1,0:T(8,128)(2,1)} %pad.20.spectra_past, bf16[8,256,256]{2,1,0:T(8,128)(2,1)} %self_inverse.1, ...), custom_call_target="tpu_custom_call" | custom-call | tf_op jit(solution)/shard_map/pallas_call | solution.py:411
  167.0 3.1 %copy.38 = bf16[4,8,256,128]{3,2,1,0:T(8,128)(2,1)} copy(bf16[4,8,256,128]{3,2,1,0:T(8,128)(2,1)} %shard_map.127) | data formatting | bytes 4194304
  (5 shorter events, 0.0 us)
Async XLA Ops:
  0.0 7.3 %copy-start.1 = (bf16[2,1,1152,128]{3,2,1,0:T(8,128)(2,1)S(1)}, bf16[2,1,1152,128]{3,2,1,0:T(8,128)(2,1)}, u32[]{:S(2)}) copy-start(bf16[2,1,1152,128]{3,2,1,0:T(8,128)(2,1)} %param.15) | copy-start | bytes 1769476
  4.0 9.2 %copy-start.2 = (bf16[256,1152]{1,0:T(8,128)(2,1)S(1)}, bf16[256,1152]{1,0:T(8,128)(2,1)}, u32[]{:S(2)}) copy-start(bf16[256,1152]{1,0:T(8,128)(2,1)} %param.20) | copy-start | bytes 1769476
  6.4 8.1 %copy-start = (f32[32,48,8]{2,1,0:T(8,128)}, f32[32,48,8]{2,1,0:T(8,128)S(1)}, u32[]{:S(2)}) copy-start(f32[32,48,8]{2,1,0:T(8,128)S(1)} %pad.23) | copy-start | bytes 147460
  6.4 8.1 %copy-start.3 = (bf16[1152,256]{1,0:T(8,128)(2,1)S(1)}, bf16[1152,256]{1,0:T(8,128)(2,1)}, u32[]{:S(2)}) copy-start(bf16[1152,256]{1,0:T(8,128)(2,1)} %param.21) | copy-start | bytes 1769476
where the time goes:
time: 173 us; the launch traced here: 170 us
  Pallas kernels  151 us (87%)
  local copies, waits for them, and re-layouts  15.9 us (9%)
  other arithmetic  3.04 us (2%)
    pallas_call x1, Pallas kernels, on_device(): pl.pallas_call(functools.partial(march, sizes), out_shape=jax.ShapeDtypeS...  151 us
    unnamed x10, local copies, waits for them, and re-layouts  8.03 us

commit v1 on v0

--- a/solution.py
+++ b/solution.py
@@ -48,7 +48,7 @@
     depth = padded // TILE
     parents = devices
     wide = parents * TILE
-    chunk = 8
+    chunk = 16
     me = lax.axis_index("grp") * per_row + lax.axis_index("dir")
 
     def place(device):
@@ -308,23 +308,25 @@
         target, base = (curs[slot], groups) if step + 1 < steps else (last, 0)
         received = arrived[step][...].reshape(devices * padded, -1)
 
-        def solve(g, carry, target=target, base=base, received=received):
-            drive = (acc[g] - dot(test[g], received)).astype(jnp.bfloat16)
-            target[base + g] = dot(inverse[g], drive).astype(jnp.bfloat16)
-            return carry
-
-        lax.fori_loop(0, groups, solve, 0)
+        def solve(both, carry, target=target, base=base, received=received):
+            tests = test[pl.ds(2 * both, 2)].reshape(2 * unknowns, received.shape[0])
+            far = dot(tests, received)
+            for half in range(2):
+                g = 2 * both + half
+                drive = acc[g] - far[half * unknowns : (half + 1) * unknowns]
+                target[base + g] = dot(inverse[g], drive.astype(jnp.bfloat16)).astype(jnp.bfloat16)
+            return carry
+
+        lax.fori_loop(0, groups // 2, solve, 0)
         own = target.at[pl.ds(base, groups)]
         results.append(pltpu.make_async_copy(own, out.at[step], out_sem.at[step]))
         if step + 1 < steps:
+            outgoing(step, slot)
             start_neighbours(own, slot)
-            outgoing(step, slot)
         results[-1].start()
     for slot in range(times):
         drain(bands[slot], band_send.at[slot])
         finish_neighbours(slot)
-        if slot == times - 1:
-            pass
     for step in range(steps):
         drain(arrived[step], inc_send.at[step])
         results[step].wait()

time: 173 us -> 165 us (0.954); the launches traced: 170 us -> 164 us
  Pallas kernels: 151 us -> 145 us
    pallas_call x1, Pallas kernels: 151 us -> 145 us  [on_device(): pl.pallas_call(functools.partial(march, sizes), out_shape=jax.ShapeDtypeS...]
where the time goes in v1:
time: 165 us; the launch traced here: 164 us
  Pallas kernels  145 us (88%)
  local copies, waits for them, and re-layouts  15.9 us (10%)
  other arithmetic  3.04 us (2%)
    pallas_call x1, Pallas kernels, on_device(): pl.pallas_call(functools.partial(march, sizes), out_shape=jax.ShapeDtypeS...  145 us
    unnamed x10, local copies, waits for them, and re-layouts  8.03 us

profile of v1, /device:TPU:16, one launch (start us, length us, event | category | flops | bytes accessed | tf_op | source)
XLA Modules:
  0.0 164.2 jit_solution(5101274912626241608)
XLA Ops:
  0.0 1.4 subtract_select_fusion.table
  1.4 0.7 add_bitcast_fusion
  2.1 0.9 reshape.26
  3.0 1.0 convert.5
  4.0 0.0 copy-start.2
  4.0 0.3 copy.34
  4.3 0.8 pad.24.factors
  5.1 0.9 copy.36.slots
  6.0 0.3 copy.33
  6.3 0.1 pad.23
  6.4 0.0 copy-start.3
  6.4 0.9 copy.35.shift_rows
  7.3 4.9 %copy.29 = bf16[2,1,1152,128]{3,0,2,1:T(2,128)(2,1)S(1)} copy(bf16[2,1,1152,128]{3,2,1,0:T(8,128)(2,1)S(1)} %copy-done.1) | data formatting | bytes 1179648 | tf_op args[2]
  12.2 0.1 copy.30
  12.3 1.0 pad.20.spectra_past
  13.2 0.2 copy.31
  13.5 0.1 reshape.22
  13.6 1.0 pad.21
  14.5 0.0 copy-done
  14.5 0.1 reshape.24
  14.7 0.1 pad.22
  14.7 1.2 copy.32
  15.9 145.2 %shard_map.127 = bf16[4,8,256,128]{3,2,1,0:T(8,128)(2,1)} custom-call(s32[8,6]{1,0:T(8,128)} %subtract_select_fusion.table, f32[4,8,256,128]{3,2,1,0:T(8,128)} %incident.1, bf16[2,8,256,128]{3,2,1,0:T(8,128)(2,1)} %currents_past.1, bf16[2,32,48,128]{3,2,1,0:T(8,128)(2,1)} %pad.20.spectra_past, bf16[8,256,256]{2,1,0:T(8,128)(2,1)} %self_inverse.1, ...), custom_call_target="tpu_custom_call" | custom-call | tf_op jit(solution)/shard_map/pallas_call | solution.py:413
  161.1 3.1 %copy.38 = bf16[4,8,256,128]{3,2,1,0:T(8,128)(2,1)} copy(bf16[4,8,256,128]{3,2,1,0:T(8,128)(2,1)} %shard_map.127) | data formatting | bytes 4194304
  (5 shorter events, 0.0 us)
Async XLA Ops:
  0.0 7.3 %copy-start.1 = (bf16[2,1,1152,128]{3,2,1,0:T(8,128)(2,1)S(1)}, bf16[2,1,1152,128]{3,2,1,0:T(8,128)(2,1)}, u32[]{:S(2)}) copy-start(bf16[2,1,1152,128]{3,2,1,0:T(8,128)(2,1)} %param.15) | copy-start | bytes 1769476
  4.0 9.2 %copy-start.2 = (bf16[256,1152]{1,0:T(8,128)(2,1)S(1)}, bf16[256,1152]{1,0:T(8,128)(2,1)}, u32[]{:S(2)}) copy-start(bf16[256,1152]{1,0:T(8,128)(2,1)} %param.20) | copy-start | bytes 1769476
  6.4 8.1 %copy-start = (f32[32,48,8]{2,1,0:T(8,128)}, f32[32,48,8]{2,1,0:T(8,128)S(1)}, u32[]{:S(2)}) copy-start(f32[32,48,8]{2,1,0:T(8,128)S(1)} %pad.23) | copy-start | bytes 147460
  6.4 8.1 %copy-start.3 = (bf16[1152,256]{1,0:T(8,128)(2,1)S(1)}, bf16[1152,256]{1,0:T(8,128)(2,1)}, u32[]{:S(2)}) copy-start(bf16[1152,256]{1,0:T(8,128)(2,1)} %param.21) | copy-start | bytes 1769476

commit v2 on v1

--- a/solution.py
+++ b/solution.py
@@ -296,11 +296,14 @@
         oldest = newest - 1
         if step == 0:
             drain(bands[oldest], band_recv.at[oldest])
-            wait_neighbours(oldest)
-        near_part(oldest, 1, step, True)
+        else:
+            near_part(oldest, 1, step, True)
         translate(step, [newest, oldest], 1, False)
         drain(bands[newest], band_recv.at[newest])
         translate(step, [newest, oldest], 0, True)
+        if step == 0:
+            wait_neighbours(oldest)
+            near_part(oldest, 1, step, True)
         wait_neighbours(newest)
         near_part(newest, 0, step, False)
         drain(arrived[step], inc_recv.at[step])

time: 165 us -> 164 us (level)
  no operation moved by 1% of the time
where the time goes in v2:
time: 164 us; the launch traced here: 163 us
  Pallas kernels  144 us (88%)
  local copies, waits for them, and re-layouts  15.9 us (10%)
  other arithmetic  3.04 us (2%)
    pallas_call x1, Pallas kernels, on_device(): pl.pallas_call(functools.partial(march, sizes), out_shape=jax.ShapeDtypeS...  144 us
    unnamed x10, local copies, waits for them, and re-layouts  8.03 us

profile of v2, /device:TPU:16, one launch (start us, length us, event | category | flops | bytes accessed | tf_op | source)
XLA Modules:
  0.0 163.5 jit_solution(16065711230838799728)
XLA Ops:
  0.0 1.4 subtract_select_fusion.table
  1.4 0.7 add_bitcast_fusion
  2.1 0.9 reshape.26
  3.0 1.0 convert.5
  4.0 0.0 copy-start.2
  4.0 0.3 copy.34
  4.3 0.8 pad.24.factors
  5.1 0.9 copy.36.slots
  6.0 0.3 copy.33
  6.3 0.1 pad.23
  6.4 0.0 copy-start.3
  6.4 0.9 copy.35.shift_rows
  7.3 4.9 %copy.29 = bf16[2,1,1152,128]{3,0,2,1:T(2,128)(2,1)S(1)} copy(bf16[2,1,1152,128]{3,2,1,0:T(8,128)(2,1)S(1)} %copy-done.1) | data formatting | bytes 1179648 | tf_op args[2]
  12.2 0.1 copy.30
  12.3 1.0 pad.20.spectra_past
  13.2 0.2 copy.31
  13.5 0.1 reshape.22
  13.6 1.0 pad.21
  14.5 0.0 copy-done
  14.5 0.1 reshape.24
  14.7 0.1 pad.22
  14.7 1.2 copy.32
  15.9 144.4 %shard_map.127 = bf16[4,8,256,128]{3,2,1,0:T(8,128)(2,1)} custom-call(s32[8,6]{1,0:T(8,128)} %subtract_select_fusion.table, f32[4,8,256,128]{3,2,1,0:T(8,128)} %incident.1, bf16[2,8,256,128]{3,2,1,0:T(8,128)(2,1)} %currents_past.1, bf16[2,32,48,128]{3,2,1,0:T(8,128)(2,1)} %pad.20.spectra_past, bf16[8,256,256]{2,1,0:T(8,128)(2,1)} %self_inverse.1, ...), custom_call_target="tpu_custom_call" | custom-call | tf_op jit(solution)/shard_map/pallas_call | solution.py:416
  160.3 3.1 %copy.38 = bf16[4,8,256,128]{3,2,1,0:T(8,128)(2,1)} copy(bf16[4,8,256,128]{3,2,1,0:T(8,128)(2,1)} %shard_map.127) | data formatting | bytes 4194304
  (5 shorter events, 0.0 us)
Async XLA Ops:
  0.0 7.3 %copy-start.1 = (bf16[2,1,1152,128]{3,2,1,0:T(8,128)(2,1)S(1)}, bf16[2,1,1152,128]{3,2,1,0:T(8,128)(2,1)}, u32[]{:S(2)}) copy-start(bf16[2,1,1152,128]{3,2,1,0:T(8,128)(2,1)} %param.15) | copy-start | bytes 1769476
  4.0 9.2 %copy-start.2 = (bf16[256,1152]{1,0:T(8,128)(2,1)S(1)}, bf16[256,1152]{1,0:T(8,128)(2,1)}, u32[]{:S(2)}) copy-start(bf16[256,1152]{1,0:T(8,128)(2,1)} %param.20) | copy-start | bytes 1769476
  6.4 8.1 %copy-start = (f32[32,48,8]{2,1,0:T(8,128)}, f32[32,48,8]{2,1,0:T(8,128)S(1)}, u32[]{:S(2)}) copy-start(f32[32,48,8]{2,1,0:T(8,128)S(1)} %pad.23) | copy-start | bytes 147460
  6.4 8.1 %copy-start.3 = (bf16[1152,256]{1,0:T(8,128)(2,1)S(1)}, bf16[1152,256]{1,0:T(8,128)(2,1)}, u32[]{:S(2)}) copy-start(bf16[1152,256]{1,0:T(8,128)(2,1)} %param.21) | copy-start | bytes 1769476
